TPU v7x, 256 devices: a whole 4x4x8 slice. The times are simulated.
256 devices in a mesh: leaf: 16 (over z, core), front: 16 (over x, y).
Axes of the slice: x: 4, y: 4, z: 8, core: 2. Of those that a mesh axis runs over, the one named last changes fastest.
Arguments:
- rhs_leaf: float32 [16, 1024, 256], P('leaf', 'front'), may hold values from -6 to 6
- rhs_top: float32 [15, 1024, 256], P(None, 'front'), may hold values from -6 to 6
- inv_leaf: bfloat16 [16, 1024, 1024], P('leaf', 'front'), as said below
- inv_top: bfloat16 [15, 1024, 1024], P(None, 'front'), as said below
- off_leaf: bfloat16 [16, 1024, 1024], P('leaf', None, 'front'), may hold values from -0.09375 to 0.09375
- off_top: bfloat16 [14, 1024, 1024], P(None, None, 'front'), may hold values from -0.09375 to 0.09375
- idx_leaf: int32 [16, 1024], P('leaf'), may hold values from 0 to 4095, as said below
- idx_top: int32 [14, 1024], replicated, may hold values from 0 to 3071, as said below
Outputs:
- leaf_solution: float32 [16, 1024, 256], P('leaf', 'front')
- ancestor_solution: float32 [16, 4, 1024, 256], P('leaf', None, 'front')
Inputs may be any that keep to these rules, and one draw needn't show every extreme that they name: `idx_leaf`: entry r of row g is a * 1024 + q with a < 4: update row r of split-level front g lands on row q of its depth-a ancestor. `idx_top`: row j belongs to the upper front with heap number h = j + 2; its entries are a * 1024 + q with a < floor(log2 h): update row r lands on row q of h's depth-a ancestor. `inv_leaf`: every block is lower triangular with a positive diagonal. `inv_top`: every block is lower triangular with a positive diagonal.
All inputs are finite; a program needn't handle non-finite values.
Results may differ from a plain program's by a relative error of at most 0.0055.
Values may be sent and summed in bfloat16 or wider, within the bound.
No kernel may reach another device: no remote copies, remote signals or barrier semaphores. Data moves between devices by JAX's collectives and lax.ppermute only.
A program may use at most 64 MiB of HBM per device.

v0:
```python
import jax
import jax.numpy as jnp
from jax import lax
from jax.sharding import PartitionSpec as P


def partner(block, axis, stride):
    count = lax.axis_size(axis)
    route = []
    for low in range(count):
        high = low | 1 << stride
        if high != low and high < count:
            route += [(low, high), (high, low)]
    return lax.ppermute(block, axis, route)


def local(rhs_leaf, rhs_top, inv_leaf, inv_top, off_leaf, off_top, idx_leaf, idx_top):
    front_width = inv_leaf.shape[2]
    rhs_count = rhs_leaf.shape[2]
    leaves = lax.axis_size("leaf")
    depth_count = leaves.bit_length() - 1
    leaf_pos = lax.axis_index("leaf")

    def apply_inverse(inverse, right_side):
        rounded = right_side.astype(jnp.bfloat16)
        return jnp.dot(
            inverse,
            lax.all_gather(rounded, "front", axis=0, tiled=True),
            preferred_element_type=jnp.float32,
        )

    def spread(off_block, solution, row_list, count):
        partial_value = jnp.dot(
            off_block, solution.astype(jnp.bfloat16), preferred_element_type=jnp.float32
        )
        dense_rows = jax.ops.segment_sum(partial_value, row_list, num_segments=count * front_width)
        dense_rows = dense_rows.reshape(count, front_width, rhs_count)
        return lax.psum_scatter(dense_rows, "front", scatter_dimension=1, tiled=True)

    leaf_solution = apply_inverse(inv_leaf[0], rhs_leaf[0])
    pending = spread(off_leaf[0], leaf_solution, idx_leaf[0], depth_count)
    solved = []
    for section_num in range(depth_count):
        pending = pending + partner(pending, "leaf", section_num)
        heap_node = jnp.right_shift(leaves + leaf_pos, section_num + 1)
        right_side = (
            lax.dynamic_index_in_dim(rhs_top, heap_node - 1, 0, keepdims=False) - pending[0]
        )
        inverse = lax.dynamic_index_in_dim(inv_top, heap_node - 1, 0, keepdims=False)
        solution = apply_inverse(inverse, right_side)
        solved.append(solution)
        if section_num + 1 < depth_count:
            off_block = lax.dynamic_index_in_dim(off_top, heap_node - 2, 0, keepdims=False)
            row_list = lax.dynamic_index_in_dim(idx_top, heap_node - 2, 0, keepdims=False)
            pending = pending[1:] + spread(
                off_block, solution, row_list, depth_count - section_num - 1
            )
    return (leaf_solution[None], jnp.stack(solved)[None])


def solution(mesh):
    placed = (
        P("leaf", "front", None),
        P(None, "front", None),
        P("leaf", "front", None),
        P(None, "front", None),
        P("leaf", None, "front"),
        P(None, None, "front"),
        P("leaf", None),
        P(),
    )
    return jax.shard_map(
        local,
        mesh=mesh,
        in_specs=placed,
        out_specs=(P("leaf", "front", None), P("leaf", None, "front", None)),
        check_vma=False,
    )
```

profile of v0, /device:TPU:32, one launch (start us, length us, event | category | flops | bytes accessed | tf_op | source)
XLA Modules:
  0.0 521.0 jit_solution(1386196292948095497)
XLA Ops:
  8.2 24.3 %all-gather = bf16[1,1024,256]{2,1,0:T(8,128)(2,1)S(1)} all-gather(bf16[1,64,256]{2,1,0:T(8,128)(2,1)S(1)} %convert_element_type.42), channel_id=2, replica_groups=mesh['leaf'=16,'front'=16] {'front'}, dimensions={1}, use_global_device_ids=true | all-gather | bytes 557056 | tf_op jit(solution)/shard_map/all_gather | solution.py:28
  32.5 1.1 fusion.13
  33.6 1.2 convolution_bitcast_fusion
  34.8 1.3 copy.10
  36.1 8.7 %scatter_custom_fusion = f32[4096,256]{1,0:T(8,128)} fusion(s32[1024]{0:T(1024)} %bitcast.71, f32[1024,256]{1,0:T(8,128)} %copy.10, f32[]{:T(128)} %constant.69.clone.1), kind=kCustom, calls=%fused_computation.4 | custom fusion | flops 262144 | bytes 4194816 | tf_op jit(solution)/shard_map/scatter-add | solution.py:36
  44.9 83.3 %reduce-scatter.5.cloned.1.call-done = f32[4,64,256]{2,1,0:T(8,128)} async-done(((f32[4,1024,256]{2,1,0:T(8,128)}), f32[4,64,256]{2,1,0:T(8,128)}) %reduce-scatter.5.cloned.1.call-update) | async-done | bytes 262160 | tf_op jit(solution)/shard_map/reduce_scatter | solution.py:38
  131.8 23.3 %all-gather.1 = bf16[1,1024,256]{2,1,0:T(8,128)(2,1)S(1)} all-gather(bf16[1,64,256]{2,1,0:T(8,128)(2,1)S(1)} %fusion.38), channel_id=3, replica_groups=mesh['leaf'=16,'front'=16] {'front'}, dimensions={1}, use_global_device_ids=true | all-gather | bytes 557056 | tf_op jit(solution)/shard_map/all_gather | solution.py:28
  155.2 1.2 fusion.23
  156.5 7.9 %scatter_custom_fusion.1 = f32[3072,256]{1,0:T(8,128)} fusion(s32[1024]{0:T(1024)S(1)} %bitcast.70, f32[1024,256]{1,0:T(8,128)S(1)} %fusion.23, f32[]{:T(128)} %constant.69.clone.1), kind=kCustom, calls=%fused_computation.6 | custom fusion | flops 262144 | bytes 3145732 | tf_op jit(solution)/shard_map/scatter-add | solution.py:36
  164.4 79.7 %reduce-scatter.7.cloned.1.call-done = f32[3,64,256]{2,1,0:T(8,128)} async-done(((f32[3,1024,256]{2,1,0:T(8,128)}), f32[3,64,256]{2,1,0:T(8,128)}) %reduce-scatter.7.cloned.1.call-update) | async-done | bytes 196624 | tf_op jit(solution)/shard_map/reduce_scatter | solution.py:38
  245.6 5.2 collective-permute-done.1
  251.7 23.5 %all-gather.2 = bf16[1,1024,256]{2,1,0:T(8,128)(2,1)S(1)} all-gather(bf16[1,64,256]{2,1,0:T(8,128)(2,1)S(1)} %fusion.37), channel_id=4, replica_groups=mesh['leaf'=16,'front'=16] {'front'}, dimensions={1}, use_global_device_ids=true | all-gather | bytes 557056 | tf_op jit(solution)/shard_map/all_gather | solution.py:28
  275.4 1.2 fusion.20
  276.7 7.5 %scatter_custom_fusion.2 = f32[2048,256]{1,0:T(8,128)} fusion(s32[1024]{0:T(1024)S(1)} %bitcast.69, f32[1024,256]{1,0:T(8,128)S(1)} %fusion.20, f32[]{:T(128)} %constant.69.clone.1), kind=kCustom, calls=%fused_computation.10 | custom fusion | flops 262144 | bytes 2097156 | tf_op jit(solution)/shard_map/scatter-add | solution.py:36
  284.2 78.2 %reduce-scatter.9.cloned.1.call-done = f32[2,64,256]{2,1,0:T(8,128)} async-done(((f32[2,1024,256]{2,1,0:T(8,128)}), f32[2,64,256]{2,1,0:T(8,128)}) %reduce-scatter.9.cloned.1.call-update) | async-done | bytes 131088 | tf_op jit(solution)/shard_map/reduce_scatter | solution.py:38
  363.3 2.6 collective-permute-start.2
  365.9 3.8 collective-permute-done.2
  370.6 23.2 %all-gather.3 = bf16[1,1024,256]{2,1,0:T(8,128)(2,1)S(1)} all-gather(bf16[1,64,256]{2,1,0:T(8,128)(2,1)S(1)} %fusion.36), channel_id=5, replica_groups=mesh['leaf'=16,'front'=16] {'front'}, dimensions={1}, use_global_device_ids=true | all-gather | bytes 557056 | tf_op jit(solution)/shard_map/all_gather | solution.py:28
  394.1 1.2 fusion.17
  395.3 7.1 %scatter_custom_fusion.3 = f32[1024,256]{1,0:T(8,128)} fusion(s32[1024]{0:T(1024)S(1)} %bitcast.68, f32[1024,256]{1,0:T(8,128)S(1)} %fusion.17, f32[]{:T(128)} %constant.69.clone.1), kind=kCustom, calls=%fused_computation.21 | custom fusion | flops 262144 | bytes 1048580 | tf_op jit(solution)/shard_map/scatter-add | solution.py:36
  402.4 77.7 %reduce-scatter.11.cloned.1.call-done = f32[1,64,256]{2,1,0:T(8,128)} async-done(((f32[1,1024,256]{2,1,0:T(8,128)}), f32[1,64,256]{2,1,0:T(8,128)}) %reduce-scatter.11.cloned.1.call-update) | async-done | bytes 65552 | tf_op jit(solution)/shard_map/reduce_scatter | solution.py:38
  480.9 5.0 collective-permute-start.3
  485.9 3.4 collective-permute-done.3
  490.2 23.3 %all-gather.4 = bf16[1,1024,256]{2,1,0:T(8,128)(2,1)S(1)} all-gather(bf16[1,64,256]{2,1,0:T(8,128)(2,1)S(1)} %subtract_convert_fusion), channel_id=6, replica_groups=mesh['leaf'=16,'front'=16] {'front'}, dimensions={1}, use_global_device_ids=true | all-gather | bytes 557056 | tf_op jit(solution)/shard_map/all_gather | solution.py:28
  (32 shorter events, 12.3 us)
Async XLA Ops:
  7.2 147.9 %copy-start = (bf16[15,64,1024]{2,1,0:T(8,128)(2,1)S(1)}, bf16[15,64,1024]{2,1,0:T(8,128)(2,1)}, u32[]{:S(2)}) copy-start(bf16[15,64,1024]{2,1,0:T(8,128)(2,1)} %param.11) | copy-start | bytes 5898244
  7.2 121.0 %reduce-scatter.5.cloned.1.call-start = ((), (), s32[]{:S(2)}) async-start(), calls=%async_computation.4 | async-start | bytes 4456448 | tf_op jit(solution)/shard_map/reduce_scatter | solution.py:38
  33.6 11.2 %copy-start.1 = (f32[64,256]{1,0:T(8,128)}, f32[64,256]{1,0:T(8,128)S(1)}, u32[]{:S(2)}) copy-start(f32[64,256]{1,0:T(8,128)S(1)} %fusion.13) | copy-start | bytes 196612
  44.8 199.3 %reduce-scatter.7.cloned.1.call-start = ((), (), s32[]{:S(2)}) async-start(), calls=%async_computation.5 | async-start | bytes 3342336 | tf_op jit(solution)/shard_map/reduce_scatter | solution.py:38
  128.2 1.7 collective-permute-start
  164.4 198.0 %reduce-scatter.9.cloned.1.call-start = ((), (), s32[]{:S(2)}) async-start(), calls=%async_computation.6 | async-start | bytes 2228224 | tf_op jit(solution)/shard_map/reduce_scatter | solution.py:38
  245.1 5.8 %collective-permute-start.1 = (f32[3,64,256]{2,1,0:T(8,128)S(1)}, f32[3,64,256]{2,1,0:T(8,128)S(1)}, u32[]{:S(2)}, u32[]{:S(2)}) collective-permute-start(f32[3,64,256]{2,1,0:T(8,128)S(1)} %slice_add_fusion), channel_id=1, source_target_pairs={{0,32},{32,0},{16,48},{48,16},{64,96},{96,64},{80,112},{112,80},{1... | collective-permute-start | bytes 589832 | tf_op jit(solution)/shard_map/ppermute | solution.py:14
  284.2 195.9 %reduce-scatter.11.cloned.1.call-start = ((), (), s32[]{:S(2)}) async-start(), calls=%async_computation.7 | async-start | bytes 1114112 | tf_op jit(solution)/shard_map/reduce_scatter | solution.py:38
  363.3 6.5 %collective-permute-start.2 = (f32[2,64,256]{2,1,0:T(8,128)S(1)}, f32[2,64,256]{2,1,0:T(8,128)S(1)}, u32[]{:S(2)}, u32[]{:S(2)}) collective-permute-start(f32[2,64,256]{2,1,0:T(8,128)S(1)} %slice_add_fusion.1), channel_id=1, source_target_pairs={{0,64},{64,0},{16,80},{80,16},{32,96},{96,32},{48,112},{112,48},{1... | collective-permute-start | bytes 393224 | tf_op jit(solution)/shard_map/ppermute | solution.py:14
  480.9 8.4 %collective-permute-start.3 = (f32[1,64,256]{2,1,0:T(8,128)S(1)}, f32[1,64,256]{2,1,0:T(8,128)S(1)}, u32[]{:S(2)}, u32[]{:S(2)}) collective-permute-start(f32[1,64,256]{2,1,0:T(8,128)S(1)} %slice_add_fusion.2), channel_id=1, source_target_pairs={{0,128},{128,0},{16,144},{144,16},{32,160},{160,32},{48,176},{176,... | collective-permute-start | bytes 196616 | tf_op jit(solution)/shard_map/ppermute | solution.py:14
Sparse Core Ops, SparseCore 0:
  45.0 83.1 reduce-scatter.4
  164.5 79.5 reduce-scatter.6
  284.3 78.0 reduce-scatter.8
  402.5 77.5 reduce-scatter.10
where the time goes:
time: 522 us; the launch traced here: 521 us
  waiting for transfers between devices  332 us (64%)
  blocking collectives  118 us (23%)
  other arithmetic  39.9 us (8%)
  between operations  13.9 us (3%)
  starting transfers between devices  8.32 us (2%)
  matrix products  6.91 us (1%)
    reduce_scatter x4, waiting for transfers between devices, spread(): lax.psum_scatter(dense_rows, 'front', scatter_dimension=1, tiled=True)  319 us
    all_gather x5, blocking collectives, apply_inverse(): lax.all_gather(rounded, 'front', axis=0, tiled=True)  118 us
    scatter-add x4, other arithmetic, spread(): jax.ops.segment_sum(partial_value, row_list, num_segments=count * front_w...  31.1 us
    ppermute x4, waiting for transfers between devices, partner(): return lax.ppermute(block, axis, route)  13.3 us
  transfers between devices with their start and end apart: 8, of which 8 were waited for; matrix products, arithmetic and copies ran while one was open for 0% of the time, Pallas kernels for 0%

commit v1 on v0

--- a/solution.py
+++ b/solution.py
@@ -23,10 +23,35 @@
 
     def apply_inverse(inverse, right_side):
         rounded = right_side.astype(jnp.bfloat16)
+
+        def group_rings_on_mesh(z, mesh_dim):
+            tall = lax.psum(1, axis_name=mesh_dim)
+            wide_out = lax.axis_index(mesh_dim)
+            reached, block_now, answer = (tall, wide_out, z.shape[0])
+            cards = list(map(lambda i: (i, (i + 1) % reached), range(reached)))
+            w1 = range(reached)
+            taken_in = map(lambda i: (i, (i - 1) % reached), w1)
+            n_now = jnp.zeros((*z.shape[:0], reached * answer, *z.shape[1:]), z.dtype)
+            n_now = lax.dynamic_update_slice_in_dim(n_now, z, block_now * answer, axis=0)
+            pages = list(taken_in)
+            k_now = reached // 2
+            ix = 1
+            opened = current_block = z
+            while ix < k_now + 1:
+                opened = lax.ppermute(opened, mesh_dim, cards)
+                n_now = lax.dynamic_update_slice_in_dim(
+                    n_now, opened, (block_now - ix) % reached * answer, axis=0
+                )
+                if ix < reached - k_now:
+                    current_block = lax.ppermute(current_block, perm=pages, axis_name=mesh_dim)
+                    n_now = lax.dynamic_update_slice_in_dim(
+                        n_now, current_block, (block_now + ix) % reached * answer, axis=0
+                    )
+                ix = ix + 1
+            return n_now
+
         return jnp.dot(
-            inverse,
-            lax.all_gather(rounded, "front", axis=0, tiled=True),
-            preferred_element_type=jnp.float32,
+            inverse, group_rings_on_mesh(rounded, "front"), preferred_element_type=jnp.float32
         )
 
     def spread(off_block, solution, row_list, count):

time: 522 us -> 693 us (1.33); the launches traced: 521 us -> 684 us
  starting transfers between devices: 8.32 us -> 200 us
  blocking collectives: 118 us -> 0 us
  waiting for transfers between devices: 332 us -> 421 us
    ppermute x0 -> x75, starting transfers between devices: none -> 192 us  [the longest x35 184 us: group_rings_on_mesh(): current_block = lax.ppermute(current_block, perm=pages, axis_name=mesh_dim)]
    all_gather x5 -> x0, blocking collectives: 118 us -> none  [apply_inverse(): lax.all_gather(rounded, 'front', axis=0, tiled=True)]
    ppermute x0 -> x75, waiting for transfers between devices: none -> 98.1 us  [the longest x40 94.6 us: group_rings_on_mesh(): opened = lax.ppermute(opened, mesh_dim, cards)]
    reduce_scatter x4, waiting for transfers between devices: 319 us -> 309 us  [spread(): lax.psum_scatter(dense_rows, 'front', scatter_dimension=1, tiled=True)]
  transfers between devices with their start and end apart: 8 -> 83, of which waited for: 8 -> 55; matrix products, arithmetic and copies ran while one was open for 0% -> 0% of each run, Pallas kernels for 0% -> 0%
where the time goes in v1:
time: 693 us; the launch traced here: 684 us
  waiting for transfers between devices  421 us (61%)
  starting transfers between devices  200 us (29%)
  other arithmetic  40 us (6%)
  between operations  14.6 us (2%)
    reduce_scatter x4, waiting for transfers between devices, spread(): lax.psum_scatter(dense_rows, 'front', scatter_dimension=1, tiled=True)  309 us
    ppermute x35, starting transfers between devices, group_rings_on_mesh(): current_block = lax.ppermute(current_block, perm=pages, axis_name=mesh_dim)  184 us
    ppermute x40, waiting for transfers between devices, group_rings_on_mesh(): opened = lax.ppermute(opened, mesh_dim, cards)  94.6 us
    scatter-add x4, other arithmetic, spread(): jax.ops.segment_sum(partial_value, row_list, num_segments=count * front_w...  31.1 us
    ppermute x4, waiting for transfers between devices, partner(): return lax.ppermute(block, axis, route)  14.2 us
  transfers between devices with their start and end apart: 83, of which 55 were waited for; matrix products, arithmetic and copies ran while one was open for 0% of the time, Pallas kernels for 0%

profile of v1, /device:TPU:32, one launch (start us, length us, event | category | flops | bytes accessed | tf_op | source)
XLA Modules:
  0.0 684.2 jit_solution(6425564555205140837)
XLA Ops:
  59.1 7.2 %collective-permute-done.14 = bf16[64,256]{1,0:T(8,128)(2,1)S(1)} collective-permute-done((bf16[64,256]{1,0:T(8,128)(2,1)S(1)}, bf16[64,256]{1,0:T(8,128)(2,1)S(1)}, u32[]{:S(2)}, u32[]{:S(2)}) %collective-permute-start.14) | collective-permute-done | bytes 32800 | tf_op jit(solution)/shard_map/ppermute | solution.py:41
  68.2 8.7 %scatter_custom_fusion = f32[4096,256]{1,0:T(8,128)} fusion(s32[1024]{0:T(1024)} %bitcast.89, f32[1024,256]{1,0:T(8,128)} %copy.10, f32[]{:T(128)} %constant.289.clone.1), kind=kCustom, calls=%fused_computation.4 | custom fusion | flops 262144 | bytes 4194816 | tf_op jit(solution)/shard_map/scatter-add | solution.py:61
  77.0 80.3 %reduce-scatter.5.cloned.1.call-done = f32[4,64,256]{2,1,0:T(8,128)} async-done(((f32[4,1024,256]{2,1,0:T(8,128)}), f32[4,64,256]{2,1,0:T(8,128)}) %reduce-scatter.5.cloned.1.call-update) | async-done | bytes 262160 | tf_op jit(solution)/shard_map/reduce_scatter | solution.py:63
  168.9 5.6 collective-permute-start.19
  176.2 5.6 collective-permute-start.21
  183.4 5.6 collective-permute-start.23
  190.6 5.6 collective-permute-start.25
  197.9 5.6 collective-permute-start.27
  205.1 5.6 collective-permute-start.29
  212.4 6.9 %collective-permute-done.30 = bf16[64,256]{1,0:T(8,128)(2,1)S(1)} collective-permute-done((bf16[64,256]{1,0:T(8,128)(2,1)S(1)}, bf16[64,256]{1,0:T(8,128)(2,1)S(1)}, u32[]{:S(2)}, u32[]{:S(2)}) %collective-permute-start.30) | collective-permute-done | bytes 32800 | tf_op jit(solution)/shard_map/ppermute | solution.py:41
  220.8 7.8 %scatter_custom_fusion.1 = f32[3072,256]{1,0:T(8,128)} fusion(s32[1024]{0:T(1024)S(1)} %bitcast.88, f32[1024,256]{1,0:T(8,128)S(1)} %fusion.15, f32[]{:T(128)} %constant.289.clone.1), kind=kCustom, calls=%fused_computation.6 | custom fusion | flops 262144 | bytes 3145732 | tf_op jit(solution)/shard_map/scatter-add | solution.py:61
  228.7 77.4 %reduce-scatter.7.cloned.1.call-done = f32[3,64,256]{2,1,0:T(8,128)} async-done(((f32[3,1024,256]{2,1,0:T(8,128)}), f32[3,64,256]{2,1,0:T(8,128)}) %reduce-scatter.7.cloned.1.call-update) | async-done | bytes 196624 | tf_op jit(solution)/shard_map/reduce_scatter | solution.py:63
  321.0 5.4 collective-permute-start.35
  343.2 5.4 collective-permute-start.41
  365.0 7.2 %collective-permute-done.46 = bf16[64,256]{1,0:T(8,128)(2,1)S(1)} collective-permute-done((bf16[64,256]{1,0:T(8,128)(2,1)S(1)}, bf16[64,256]{1,0:T(8,128)(2,1)S(1)}, u32[]{:S(2)}, u32[]{:S(2)}) %collective-permute-start.46) | collective-permute-done | bytes 32800 | tf_op jit(solution)/shard_map/ppermute | solution.py:41
  373.6 7.4 %scatter_custom_fusion.2 = f32[2048,256]{1,0:T(8,128)} fusion(s32[1024]{0:T(1024)S(1)} %bitcast.87, f32[1024,256]{1,0:T(8,128)S(1)} %fusion.11, f32[]{:T(128)} %constant.289.clone.1), kind=kCustom, calls=%fused_computation.10 | custom fusion | flops 262144 | bytes 2097156 | tf_op jit(solution)/shard_map/scatter-add | solution.py:61
  381.1 76.1 %reduce-scatter.9.cloned.1.call-done = f32[2,64,256]{2,1,0:T(8,128)} async-done(((f32[2,1024,256]{2,1,0:T(8,128)}), f32[2,64,256]{2,1,0:T(8,128)}) %reduce-scatter.9.cloned.1.call-update) | async-done | bytes 131088 | tf_op jit(solution)/shard_map/reduce_scatter | solution.py:63
  495.0 5.4 collective-permute-start.57
  517.1 7.2 %collective-permute-done.62 = bf16[64,256]{1,0:T(8,128)(2,1)S(1)} collective-permute-done((bf16[64,256]{1,0:T(8,128)(2,1)S(1)}, bf16[64,256]{1,0:T(8,128)(2,1)S(1)}, u32[]{:S(2)}, u32[]{:S(2)}) %collective-permute-start.62) | collective-permute-done | bytes 32800 | tf_op jit(solution)/shard_map/ppermute | solution.py:41
  525.7 7.1 %scatter_custom_fusion.3 = f32[1024,256]{1,0:T(8,128)} fusion(s32[1024]{0:T(1024)S(1)} %bitcast.86, f32[1024,256]{1,0:T(8,128)S(1)} %fusion.8, f32[]{:T(128)} %constant.289.clone.1), kind=kCustom, calls=%fused_computation.12 | custom fusion | flops 262144 | bytes 1048580 | tf_op jit(solution)/shard_map/scatter-add | solution.py:61
  532.8 75.4 %reduce-scatter.11.cloned.1.call-done = f32[1,64,256]{2,1,0:T(8,128)} async-done(((f32[1,1024,256]{2,1,0:T(8,128)}), f32[1,64,256]{2,1,0:T(8,128)}) %reduce-scatter.11.cloned.1.call-update) | async-done | bytes 65552 | tf_op jit(solution)/shard_map/reduce_scatter | solution.py:63
  654.9 5.6 collective-permute-start.75
  662.1 5.6 collective-permute-start.77
  669.4 7.2 %collective-permute-done.78 = bf16[64,256]{1,0:T(8,128)(2,1)S(1)} collective-permute-done((bf16[64,256]{1,0:T(8,128)(2,1)S(1)}, bf16[64,256]{1,0:T(8,128)(2,1)S(1)}, u32[]{:S(2)}, u32[]{:S(2)}) %collective-permute-start.78) | collective-permute-done | bytes 32800 | tf_op jit(solution)/shard_map/ppermute | solution.py:41
  (261 shorter events, 232.5 us)
Async XLA Ops:
  7.2 150.1 %reduce-scatter.5.cloned.1.call-start = ((), (), s32[]{:S(2)}) async-start(), calls=%async_computation.4 | async-start | bytes 4456448 | tf_op jit(solution)/shard_map/reduce_scatter | solution.py:63
  15.5 7.2 %collective-permute-start.2 = (bf16[64,256]{1,0:T(8,128)(2,1)S(1)}, bf16[64,256]{1,0:T(8,128)(2,1)S(1)}, u32[]{:S(2)}, u32[]{:S(2)}) collective-permute-start(bf16[64,256]{1,0:T(8,128)(2,1)S(1)} %collective-permute-done), channel_id=1, source_target_pairs={{0,1},{1,2},{2,3},{3,4},{4,5},{5,6},{6,7},{7,8},{8,9},{9,10},{10,1... | collective-permute-start | bytes 98312 | tf_op jit(solution)/shard_map/ppermute | solution.py:41
  22.8 7.2 %collective-permute-start.4 = (bf16[64,256]{1,0:T(8,128)(2,1)S(1)}, bf16[64,256]{1,0:T(8,128)(2,1)S(1)}, u32[]{:S(2)}, u32[]{:S(2)}) collective-permute-start(bf16[64,256]{1,0:T(8,128)(2,1)S(1)} %collective-permute-done.2), channel_id=1, source_target_pairs={{0,1},{1,2},{2,3},{3,4},{4,5},{5,6},{6,7},{7,8},{8,9},{9,10},{10,1... | collective-permute-start | bytes 98312 | tf_op jit(solution)/shard_map/ppermute | solution.py:41
  51.7 7.4 %collective-permute-start.13 = (bf16[64,256]{1,0:T(8,128)(2,1)S(1)}, bf16[64,256]{1,0:T(8,128)(2,1)S(1)}, u32[]{:S(2)}, u32[]{:S(2)}) collective-permute-start(bf16[64,256]{1,0:T(8,128)(2,1)S(1)} %collective-permute-done.11), channel_id=1, source_target_pairs={{0,15},{1,0},{2,1},{3,2},{4,3},{5,4},{6,5},{7,6},{8,7},{9,8},{10,9... | collective-permute-start | bytes 98312 | tf_op jit(solution)/shard_map/ppermute | solution.py:46
  58.9 7.4 %collective-permute-start.14 = (bf16[64,256]{1,0:T(8,128)(2,1)S(1)}, bf16[64,256]{1,0:T(8,128)(2,1)S(1)}, u32[]{:S(2)}, u32[]{:S(2)}) collective-permute-start(bf16[64,256]{1,0:T(8,128)(2,1)S(1)} %collective-permute-done.12), channel_id=1, source_target_pairs={{0,1},{1,2},{2,3},{3,4},{4,5},{5,6},{6,7},{7,8},{8,9},{9,10},{10,1... | collective-permute-start | bytes 98312 | tf_op jit(solution)/shard_map/ppermute | solution.py:41
  77.0 229.1 %reduce-scatter.7.cloned.1.call-start = ((), (), s32[]{:S(2)}) async-start(), calls=%async_computation.5 | async-start | bytes 3342336 | tf_op jit(solution)/shard_map/reduce_scatter | solution.py:63
  161.0 7.3 %collective-permute-start.16 = (bf16[64,256]{1,0:T(8,128)(2,1)S(1)}, bf16[64,256]{1,0:T(8,128)(2,1)S(1)}, u32[]{:S(2)}, u32[]{:S(2)}) collective-permute-start(bf16[64,256]{1,0:T(8,128)(2,1)S(1)} %get-tuple-element.9), channel_id=1, source_target_pairs={{0,1},{1,2},{2,3},{3,4},{4,5},{5,6},{6,7},{7,8},{8,9},{9,10},{10,1... | collective-permute-start | bytes 98312 | tf_op jit(solution)/shard_map/ppermute | solution.py:41
  197.2 7.6 %collective-permute-start.26 = (bf16[64,256]{1,0:T(8,128)(2,1)S(1)}, bf16[64,256]{1,0:T(8,128)(2,1)S(1)}, u32[]{:S(2)}, u32[]{:S(2)}) collective-permute-start(bf16[64,256]{1,0:T(8,128)(2,1)S(1)} %collective-permute-done.24), channel_id=1, source_target_pairs={{0,1},{1,2},{2,3},{3,4},{4,5},{5,6},{6,7},{7,8},{8,9},{9,10},{10,1... | collective-permute-start | bytes 98312 | tf_op jit(solution)/shard_map/ppermute | solution.py:41
  228.6 228.6 %reduce-scatter.9.cloned.1.call-start = ((), (), s32[]{:S(2)}) async-start(), calls=%async_computation.6 | async-start | bytes 2228224 | tf_op jit(solution)/shard_map/reduce_scatter | solution.py:63
  313.7 7.3 %collective-permute-start.32 = (bf16[64,256]{1,0:T(8,128)(2,1)S(1)}, bf16[64,256]{1,0:T(8,128)(2,1)S(1)}, u32[]{:S(2)}, u32[]{:S(2)}) collective-permute-start(bf16[64,256]{1,0:T(8,128)(2,1)S(1)} %get-tuple-element.7), channel_id=1, source_target_pairs={{0,1},{1,2},{2,3},{3,4},{4,5},{5,6},{6,7},{7,8},{8,9},{9,10},{10,1... | collective-permute-start | bytes 98312 | tf_op jit(solution)/shard_map/ppermute | solution.py:41
  328.3 7.6 %collective-permute-start.36 = (bf16[64,256]{1,0:T(8,128)(2,1)S(1)}, bf16[64,256]{1,0:T(8,128)(2,1)S(1)}, u32[]{:S(2)}, u32[]{:S(2)}) collective-permute-start(bf16[64,256]{1,0:T(8,128)(2,1)S(1)} %collective-permute-done.34), channel_id=1, source_target_pairs={{0,1},{1,2},{2,3},{3,4},{4,5},{5,6},{6,7},{7,8},{8,9},{9,10},{10,1... | collective-permute-start | bytes 98312 | tf_op jit(solution)/shard_map/ppermute | solution.py:41
  328.3 7.7 %collective-permute-start.37 = (bf16[64,256]{1,0:T(8,128)(2,1)S(1)}, bf16[64,256]{1,0:T(8,128)(2,1)S(1)}, u32[]{:S(2)}, u32[]{:S(2)}) collective-permute-start(bf16[64,256]{1,0:T(8,128)(2,1)S(1)} %collective-permute-done.35), channel_id=1, source_target_pairs={{0,15},{1,0},{2,1},{3,2},{4,3},{5,4},{6,5},{7,6},{8,7},{9,8},{10,9... | collective-permute-start | bytes 98312 | tf_op jit(solution)/shard_map/ppermute | solution.py:46
  335.8 7.4 %collective-permute-start.38 = (bf16[64,256]{1,0:T(8,128)(2,1)S(1)}, bf16[64,256]{1,0:T(8,128)(2,1)S(1)}, u32[]{:S(2)}, u32[]{:S(2)}) collective-permute-start(bf16[64,256]{1,0:T(8,128)(2,1)S(1)} %collective-permute-done.36), channel_id=1, source_target_pairs={{0,1},{1,2},{2,3},{3,4},{4,5},{5,6},{6,7},{7,8},{8,9},{9,10},{10,1... | collective-permute-start | bytes 98312 | tf_op jit(solution)/shard_map/ppermute | solution.py:41
  381.1 227.1 %reduce-scatter.11.cloned.1.call-start = ((), (), s32[]{:S(2)}) async-start(), calls=%async_computation.7 | async-start | bytes 1114112 | tf_op jit(solution)/shard_map/reduce_scatter | solution.py:63
  465.5 7.3 %collective-permute-start.48 = (bf16[64,256]{1,0:T(8,128)(2,1)S(1)}, bf16[64,256]{1,0:T(8,128)(2,1)S(1)}, u32[]{:S(2)}, u32[]{:S(2)}) collective-permute-start(bf16[64,256]{1,0:T(8,128)(2,1)S(1)} %get-tuple-element.5), channel_id=1, source_target_pairs={{0,1},{1,2},{2,3},{3,4},{4,5},{5,6},{6,7},{7,8},{8,9},{9,10},{10,1... | collective-permute-start | bytes 98312 | tf_op jit(solution)/shard_map/ppermute | solution.py:41
  472.8 7.4 %collective-permute-start.50 = (bf16[64,256]{1,0:T(8,128)(2,1)S(1)}, bf16[64,256]{1,0:T(8,128)(2,1)S(1)}, u32[]{:S(2)}, u32[]{:S(2)}) collective-permute-start(bf16[64,256]{1,0:T(8,128)(2,1)S(1)} %collective-permute-done.48), channel_id=1, source_target_pairs={{0,1},{1,2},{2,3},{3,4},{4,5},{5,6},{6,7},{7,8},{8,9},{9,10},{10,1... | collective-permute-start | bytes 98312 | tf_op jit(solution)/shard_map/ppermute | solution.py:41
  480.3 7.5 %collective-permute-start.52 = (bf16[64,256]{1,0:T(8,128)(2,1)S(1)}, bf16[64,256]{1,0:T(8,128)(2,1)S(1)}, u32[]{:S(2)}, u32[]{:S(2)}) collective-permute-start(bf16[64,256]{1,0:T(8,128)(2,1)S(1)} %collective-permute-done.50), channel_id=1, source_target_pairs={{0,1},{1,2},{2,3},{3,4},{4,5},{5,6},{6,7},{7,8},{8,9},{9,10},{10,1... | collective-permute-start | bytes 98312 | tf_op jit(solution)/shard_map/ppermute | solution.py:41
  480.3 7.5 %collective-permute-start.53 = (bf16[64,256]{1,0:T(8,128)(2,1)S(1)}, bf16[64,256]{1,0:T(8,128)(2,1)S(1)}, u32[]{:S(2)}, u32[]{:S(2)}) collective-permute-start(bf16[64,256]{1,0:T(8,128)(2,1)S(1)} %collective-permute-done.51), channel_id=1, source_target_pairs={{0,15},{1,0},{2,1},{3,2},{4,3},{5,4},{6,5},{7,6},{8,7},{9,8},{10,9... | collective-permute-start | bytes 98312 | tf_op jit(solution)/shard_map/ppermute | solution.py:46
  509.4 7.6 %collective-permute-start.61 = (bf16[64,256]{1,0:T(8,128)(2,1)S(1)}, bf16[64,256]{1,0:T(8,128)(2,1)S(1)}, u32[]{:S(2)}, u32[]{:S(2)}) collective-permute-start(bf16[64,256]{1,0:T(8,128)(2,1)S(1)} %collective-permute-done.59), channel_id=1, source_target_pairs={{0,15},{1,0},{2,1},{3,2},{4,3},{5,4},{6,5},{7,6},{8,7},{9,8},{10,9... | collective-permute-start | bytes 98312 | tf_op jit(solution)/shard_map/ppermute | solution.py:46
  516.7 7.6 %collective-permute-start.62 = (bf16[64,256]{1,0:T(8,128)(2,1)S(1)}, bf16[64,256]{1,0:T(8,128)(2,1)S(1)}, u32[]{:S(2)}, u32[]{:S(2)}) collective-permute-start(bf16[64,256]{1,0:T(8,128)(2,1)S(1)} %collective-permute-done.60), channel_id=1, source_target_pairs={{0,1},{1,2},{2,3},{3,4},{4,5},{5,6},{6,7},{7,8},{8,9},{9,10},{10,1... | collective-permute-start | bytes 98312 | tf_op jit(solution)/shard_map/ppermute | solution.py:41
  609.1 8.4 %collective-permute-start.63 = (f32[1,64,256]{2,1,0:T(8,128)S(1)}, f32[1,64,256]{2,1,0:T(8,128)S(1)}, u32[]{:S(2)}, u32[]{:S(2)}) collective-permute-start(f32[1,64,256]{2,1,0:T(8,128)S(1)} %slice_add_fusion.2), channel_id=1, source_target_pairs={{0,128},{128,0},{16,144},{144,16},{32,160},{160,32},{48,176},{176,... | collective-permute-start | bytes 196616 | tf_op jit(solution)/shard_map/ppermute | solution.py:14
  618.4 7.3 %collective-permute-start.64 = (bf16[64,256]{1,0:T(8,128)(2,1)S(1)}, bf16[64,256]{1,0:T(8,128)(2,1)S(1)}, u32[]{:S(2)}, u32[]{:S(2)}) collective-permute-start(bf16[64,256]{1,0:T(8,128)(2,1)S(1)} %get-tuple-element.3), channel_id=1, source_target_pairs={{0,1},{1,2},{2,3},{3,4},{4,5},{5,6},{6,7},{7,8},{8,9},{9,10},{10,1... | collective-permute-start | bytes 98312 | tf_op jit(solution)/shard_map/ppermute | solution.py:41
  632.9 7.5 %collective-permute-start.68 = (bf16[64,256]{1,0:T(8,128)(2,1)S(1)}, bf16[64,256]{1,0:T(8,128)(2,1)S(1)}, u32[]{:S(2)}, u32[]{:S(2)}) collective-permute-start(bf16[64,256]{1,0:T(8,128)(2,1)S(1)} %collective-permute-done.66), channel_id=1, source_target_pairs={{0,1},{1,2},{2,3},{3,4},{4,5},{5,6},{6,7},{7,8},{8,9},{9,10},{10,1... | collective-permute-start | bytes 98312 | tf_op jit(solution)/shard_map/ppermute | solution.py:41
  632.9 7.5 %collective-permute-start.69 = (bf16[64,256]{1,0:T(8,128)(2,1)S(1)}, bf16[64,256]{1,0:T(8,128)(2,1)S(1)}, u32[]{:S(2)}, u32[]{:S(2)}) collective-permute-start(bf16[64,256]{1,0:T(8,128)(2,1)S(1)} %collective-permute-done.67), channel_id=1, source_target_pairs={{0,15},{1,0},{2,1},{3,2},{4,3},{5,4},{6,5},{7,6},{8,7},{9,8},{10,9... | collective-permute-start | bytes 98312 | tf_op jit(solution)/shard_map/ppermute | solution.py:46
  (63 other events, 753.9 us)
Sparse Core Ops, SparseCore 0:
  77.1 80.1 reduce-scatter.4
  228.7 77.2 reduce-scatter.6
  381.2 75.9 reduce-scatter.8
  533.0 75.2 reduce-scatter.10
